TPU v7x, 256 devices: a whole 4x4x8 slice. The times are simulated.
256 devices in a mesh: orb: 16 (over z, core), slab: 16 (over y, x).
Axes of the slice: x: 4, y: 4, z: 8, core: 2. Of those that a mesh axis runs over, the one named last changes fastest.
Arguments:
- orbitals: float32 [16, 128, 48, 128], P('orb', 'slab'), may hold values from -6 to 6
- occupations: float32 [16], P('orb'), may hold values from 0.25 to 1
Outputs:
- exchange: float32 [16, 128, 48, 128], P('orb', 'slab')
All inputs are finite; a program needn't handle non-finite values.
Results may differ from a plain program's by a relative error of at most 0.0003.
Values sent between devices are 32-bit elements; how exact they have to be, the bound alone decides.
A program may use at most 128 MiB of HBM per device.

v0:
```python
import functools

import jax
import jax.numpy as jnp
import numpy as np
from jax import lax
from jax.experimental import pallas as pl
from jax.experimental.pallas import tpu as pltpu
from jax.sharding import PartitionSpec as P

MESH = pl.DeviceIdType.MESH

NZ, NY, NX = 128, 48, 128
SWEEPS = 6
screening = 0.001
relaxation = 0.8

STEP = [0.25**level for level in range(4)]
CENTRE = [6.0 * step + screening for step in STEP]
KEEP = 1.0 - relaxation
PULL = [relaxation / centre for centre in CENTRE]
SIDE = [pull * step for pull, step in zip(PULL, STEP)]

ROWS1 = 48
FINE = 64
MSG = 16
MSG2 = 24


def response_weights():
    def sides(u):
        padded = np.pad(u, ((0, 0), (1, 1), (0, 0), (0, 0)))
        return padded[:, 2:] + padded[:, :-2] + sum(np.roll(u, by, axis) for by in (1, -1) for axis in (2, 3))

    def smoothed(u, level):
        return KEEP * u + SIDE[level] * sides(u)

    def mean(u):
        b, z, y, x = u.shape
        return u.reshape(b, z // 2, 2, y // 2, 2, x // 2, 2).mean((2, 4, 6))

    def spread(u):
        return u.repeat(2, 1).repeat(2, 2).repeat(2, 3)

    unit = np.zeros((8, 8, 6, 6))
    for z in range(8):
        unit[z, z, 0, 0] = 1.0
    u = spread(smoothed(spread(unit), 1))
    u = smoothed(smoothed(u, 0), 0)
    u = mean(STEP[0] * sides(u) - CENTRE[0] * u)
    u = mean(smoothed(u, 1))
    weights = np.zeros((8, 5, 3, 3))
    for z in range(8):
        for dz in range(-2, 3):
            if 0 <= z + dz < 8:
                weights[z, dz + 2] = u[z, z + dz, :3, :3]
    return weights


def turn(value, by, axis):
    return pltpu.roll(value, by % value.shape[axis], axis)


def put(ref, slot, value):
    ref[slot, 8:56, :] = value
    ref[slot, 7:8, :] = value[47:48]
    ref[slot, 56:57, :] = value[0:1]


def lanes(rows):
    return lax.broadcasted_iota(jnp.int32, (rows, 128), 1)


def in_plane(value, lane_step):
    return (turn(value, 1, 0) + turn(value, -1, 0)) + (turn(value, lane_step, 1) + turn(value, -lane_step, 1))


def swapped(value, bit):
    first = (lanes(value.shape[0]) & bit) == 0
    return jnp.where(first, turn(value, -bit, 1), turn(value, bit, 1))


def total(parts):
    parts = [part for part in parts if part is not None]
    while len(parts) > 1:
        parts = [a + b for a, b in zip(parts[::2], parts[1::2])] + parts[len(parts) // 2 * 2 :]
    return parts[0] if parts else None


def kernel(
    n_orb, n_slab,
    occ_ref, orb_ref, out_ref,
    own, orb_x, orb_y, occ_own, occ_x, occ_y, f, v2, v, v1, pe1, f1, src1, pe2, e1, f1_out, f1_in, f2_out, f2_in, msg2, gather, gather2, e2, e2b,
    out_y, in_y, both_x, orb_n, occ_n, last, fix_out, fix_in,
    go, local_sem, orb_send, orb_recv, next_send, next_recv, gat_send, gat_recv, f1_send, f1_recv, f_send, f_recv, ret_send, ret_recv, prev_send, prev_recv, before_send, before_recv,
):
    o, s = lax.axis_index("orb"), lax.axis_index("slab")
    core = lax.rem(o, 2)
    partner = {"orb": o + 1 - 2 * core}
    before = {"orb": lax.rem(o + n_orb - 1 - core, n_orb)}
    after = {"orb": lax.rem(o + 2 - o // (n_orb - 1), n_orb)}
    start, home = o == 0, o == 1
    leads = (core == 1) & (o != 1) | (o == 0)
    above, below = lax.rem(s + 1, n_slab), lax.rem(s + n_slab - 1, n_slab)
    odd = lax.rem(s, 2)

    def at_slab(index):
        return {"slab": index}

    mine = pltpu.make_async_copy(orb_ref.at[0], own, local_sem)
    mine.start()
    peers = sorted(((x, y) for x in range(4) for y in range(4) if x or y), key=lambda d: -min(d[0], 4 - d[0]) - min(d[1], 4 - d[1]))
    peers = [4 * lax.rem(s // 4 + y, 4) + lax.rem(s + x, 4) for x, y in peers]

    barrier = pltpu.get_barrier_semaphore()

    def greet(device):
        pl.semaphore_signal(barrier, inc=1, device_id=device, device_id_type=MESH)

    greet(partner)

    @pl.when(core == 0)
    def _():
        for peer in peers:
            greet({"orb": o, "slab": peer})

    @pl.when(leads)
    def _():
        greet(before)

    @pl.when(core == 1)
    def _():
        greet({"orb": lax.rem(o + 1, n_orb)})
        for peer in peers:
            greet({"orb": o - 1, "slab": peer})

    occ_own[...] = jnp.full((8, 128), occ_ref[0], jnp.float32)
    for slot in (0, 17):
        gather[pl.ds(slot * MSG, MSG), :] = jnp.zeros((MSG, 128), jnp.float32)
    for slot in (0, 18):
        gather2[pl.ds(slot * MSG2, 2 * MSG2), :] = jnp.zeros((2 * MSG2, 128), jnp.float32)
    e2[...] = jnp.zeros_like(e2)
    e2b[...] = jnp.zeros_like(e2b)
    src1[...] = jnp.zeros_like(src1)
    low = jnp.where(s > 0, 1.0, 0.0).astype(jnp.float32)
    high = jnp.where(s < n_slab - 1, 1.0, 0.0).astype(jnp.float32)
    low2 = jnp.where(s > 1, 1.0, 0.0).astype(jnp.float32)
    high2 = jnp.where(s < n_slab - 2, 1.0, 0.0).astype(jnp.float32)

    def inside(plane, count):
        return low if plane < 0 else high if plane >= count else 1.0

    def remote(src, dst, send_sem, recv_sem, device):
        return pltpu.make_async_remote_copy(src, dst, send_sem, recv_sem, device_id=device, device_id_type=MESH)

    mine.wait()

    @pl.when(core == 0)
    def _():
        pl.semaphore_wait(barrier, 2 * n_slab)
        pl.semaphore_signal(go, inc=1, device_id=partner, device_id_type=MESH)

    @pl.when(core == 1)
    def _():
        pl.semaphore_wait(barrier, 2)

    to_next = [
        remote(own, orb_y, next_send.at[0], next_recv.at[0], after),
        remote(occ_own, occ_y, next_send.at[1], next_recv.at[1], after),
    ]
    to_partner = [
        remote(own, orb_x, orb_send.at[0], orb_recv.at[0], partner),
        remote(occ_own, occ_x, orb_send.at[1], orb_recv.at[1], partner),
    ]

    @pl.when(core == 1)
    def _():
        for copy in to_next:
            copy.start()

    @pl.when(jnp.logical_not(home))
    def _():
        for copy in to_partner:
            copy.start()

    @pl.when(start)
    def _():
        occ_x[...] = occ_own[...]
        orb_x[...] = own[...]

    @pl.when(jnp.logical_not(leads))
    def _():
        occ_y[...] = occ_own[...]
        orb_y[...] = own[...]

    @pl.when(jnp.logical_not(start))
    def _():
        for copy in to_partner:
            copy.wait_recv()

    @pl.when(leads)
    def _():
        for copy in to_next:
            copy.wait_recv()

    for p in range(8):
        put(f, 3 + p, orb_x[p] * orb_y[p])

    to_before = [
        remote(orb_x, orb_n, before_send.at[0], before_recv.at[0], before),
        remote(occ_x, occ_n, before_send.at[1], before_recv.at[1], before),
    ]

    pending = []

    def send(src, dst, send_sem, recv_sem, device):
        copy = remote(src, dst, send_sem, recv_sem, device)
        copy.start()
        pending.append(copy)
        return copy

    def restricted(pair, beyond, source, centre, side, bit):
        beyond = total([part for plane in beyond for part in plane[:2]])
        terms = []
        if pair:
            even, odd_, before, after = [total([plane[i] for plane in pair]) for i in range(4)]
            both = even + odd_
            terms.append(centre * both)
            around = total([both + both, before, after, turn(both, bit, 1), turn(both, -bit, 1), beyond])
        else:
            around = beyond
        terms.append(side * around)
        terms += [part for plane in source for part in plane]
        mean = total(terms)
        return 0.125 * (mean + swapped(mean, bit))

    def fine_rows(ref, plane):
        return [ref[plane, pl.ds(8 + start, 24, stride=2), :] for start in (0, 1, -1, 2)]

    def put_src1(slot, value):
        src1[slot, 8:32, :] = value
        src1[slot, 7:8, :] = value[23:24]
        src1[slot, 32:33, :] = value[0:1]

    def coarse_rows(slot):
        return [src1[slot, pl.ds(8 + start, MSG, stride=2), :] for start in (0, 1, -1, 2)]

    lane16 = lanes(MSG)
    place16 = (lane16 + 2 * odd) & 3

    def level2_parts(have, planes):
        parts = {}
        for d in planes:
            pair = [coarse_rows(q + 4) for q in (2 * d, 2 * d + 1) if q in have]
            beyond = [coarse_rows(q + 4) for q in (2 * d - 1, 2 * d + 2) if q in have]
            parts[d] = restricted(pair, beyond, [], KEEP, SIDE[1], 2)
        return parts

    def laid(parts, planes):
        by_place = {d % 4: parts[d] for d in planes}
        return jnp.where(place16 < 2, jnp.where(place16 == 0, by_place[0], by_place[1]), jnp.where(place16 == 2, by_place[2], by_place[3]))

    slot1 = pl.ds(pl.multiple_of((s + 1) * MSG, MSG), MSG)
    slot2 = pl.ds(pl.multiple_of((s + 2) * MSG2, MSG2), MSG2)

    def send_first(parts):
        gather[slot1, :] = laid(parts, range(-1, 3))

        @pl.when(core == 1)
        def _():
            pl.semaphore_wait(go, 1)

        for peer in peers:
            remote(gather.at[slot1], gather.at[slot1], gat_send.at[0], gat_recv.at[0], at_slab(peer)).start()

    def send_second(parts):
        msg2[0:12, :] = laid(parts, range(-1, 3))[0:12]
        msg2[12:24, :] = laid(parts, (-3, -2, 3, 4))[0:12]
        gather2[slot2, :] = msg2[...]
        for peer in peers:
            remote(msg2, gather2.at[slot2], gat_send.at[1], gat_recv.at[1], at_slab(peer)).start()

    def gathered(g):
        most = gather.at[pl.ds(0, (n_slab - 1) * MSG)] if g == 0 else gather2.at[pl.ds(0, (n_slab - 1) * MSG2)]
        return remote(most, most, gat_send.at[g], gat_recv.at[g], at_slab(above))

    row8 = lax.broadcasted_iota(jnp.int32, (8, 128), 0)
    lane8 = lanes(8)
    first_row, last_row = row8 == 0, row8 == 7

    def level2_sides(u):
        result = []
        for y in range(12):
            here = u[y]
            up = jnp.where(last_row, 0.0, turn(turn(here, 3, 1), -1, 0))
            down = jnp.where(first_row, 0.0, turn(turn(here, -3, 1), 1, 0))
            up = jnp.where((lane8 & 3) == 3, up, turn(here, -1, 1))
            down = jnp.where((lane8 & 3) == 0, down, turn(here, 1, 1))
            x = turn(here, 4, 1) + turn(here, -4, 1)
            result.append(total([u[(y + 1) % 12], u[(y + 11) % 12], up, down, x]))
        return result

    def level3_sides(u):
        result = []
        lower = (lane8 & 2) == 0
        for y in range(6):
            here = u[y]
            a, b = turn(here, -2, 1), turn(here, 2, 1)
            far = jnp.where(lower, jnp.where(first_row, 0.0, turn(a, 1, 0)), jnp.where(last_row, 0.0, turn(b, -1, 0)))
            x = turn(here, 8, 1) + turn(here, -8, 1)
            result.append(total([u[(y + 1) % 6], u[(y + 5) % 6], jnp.where(lower, a, b), far, x]))
        return result

    place8 = lane8 & 3

    def first_source():
        source = []
        for y in range(12):
            even, odd_, even_after, odd_before = [gather[pl.ds(MSG * k + y, 8, stride=2 * MSG), :] for k in (1, 2, 3, 0)]
            source.append(jnp.where(place8 == 3, even_after, even) + jnp.where(place8 == 0, odd_before, odd_))
        return source

    def second_source():
        source = []
        for y in range(12):
            even, odd_, even_after, odd_before = [gather2[pl.ds(MSG2 * k + y, 8, stride=2 * MSG2), :] for k in (2, 3, 4, 1)]
            near = jnp.where(place8 == 3, even_after, even) + jnp.where(place8 == 0, odd_before, odd_)
            even_before, even, even_after, odd_before, odd_, odd_after = [
                gather2[pl.ds(MSG2 * k + 12 + y, 8, stride=2 * MSG2), :] for k in (0, 2, 4, 1, 3, 5)]
            far = jnp.where(place8 == 0, even_before, jnp.where(place8 == 3, even, even_after))
            far = far + jnp.where(place8 == 0, odd_, jnp.where(place8 == 3, odd_after, odd_before))
            source.append(near + far)
        return source

    def response(u):
        weights = response_weights()
        plane = 4 * row8 + place8

        def weight(dz, dy, dx):
            inner = float(weights[4, dz + 2, dy, dx])
            value = inner
            for at, z in ((0, 0), (1, 1), (30, 6), (31, 7)):
                if abs(weights[z, dz + 2, dy, dx] - inner) > 1e-12:
                    value = jnp.where(plane == at, jnp.float32(weights[z, dz + 2, dy, dx]), value)
            return value

        x1 = [turn(a, 4, 1) + turn(a, -4, 1) for a in u]
        x2 = [turn(a, 8, 1) + turn(a, -8, 1) for a in u]

        def beside(a, y, by):
            return a[(y + by) % 12] + a[(y - by) % 12]

        groups = ((0, 0), (0, 1), (0, 2), (1, 1), (1, 2))
        by_dz = {dz: [weight(dz, *group) for group in groups] for dz in (-1, 0, 1)}
        two = [float(weights[4, 4, dy, dx]) for dy, dx in ((0, 0), (0, 1), (1, 1))]
        result = []
        for y in range(12):
            sums = [u[y], x1[y] + beside(u, y, 1), x2[y] + beside(u, y, 2), beside(x1, y, 1), beside(x2, y, 1) + beside(x1, y, 2)]
            here, up, down = [total([w * a for w, a in zip(by_dz[dz], sums)]) for dz in (0, -1, 1)]
            far = two[0] * sums[0] + two[1] * sums[1] + two[2] * sums[3]
            up = jnp.where(place8 == 3, jnp.where(last_row, 0.0, turn(turn(up, 3, 1), -1, 0)), turn(up, -1, 1))
            down = jnp.where(place8 == 0, jnp.where(first_row, 0.0, turn(turn(down, -3, 1), 1, 0)), turn(down, 1, 1))
            a, b = turn(far, 2, 1), turn(far, -2, 1)
            far = jnp.where(place8 >= 2, a + jnp.where(last_row, 0.0, turn(a, -1, 0)), b + jnp.where(first_row, 0.0, turn(b, 1, 0)))
            result.append(total([here, up, down, far]))
        return result

    def solve_level2(source):
        sides = level2_sides(source)
        residual = [KEEP * a + SIDE[2] * b for a, b in zip(source, sides)]
        source3 = []
        for y in range(6):
            pair = residual[2 * y] + residual[2 * y + 1]
            pair = pair + swapped(pair, 1)
            source3.append(0.125 * (pair + swapped(pair, 4)))
        pull = [PULL[3] * a for a in source3]
        iterate = pull
        for _ in range(SWEEPS - 1):
            sides = level3_sides(iterate)
            iterate = [KEEP * a + b + SIDE[3] * c for a, b, c in zip(iterate, pull, sides)]
        pull = [PULL[2] * a for a in source]
        u = [a + iterate[y // 2] for y, a in enumerate(pull)]
        sides = level2_sides(u)
        return [KEEP * a + b + SIDE[2] * c for a, b, c in zip(u, pull, sides)]

    def spread_level2(g, ds):
        row = 8 + s // 2
        a, b, c = [(e2, e2b)[g][pl.ds(row + by, MSG, stride=24), :] for by in (-1, 0, 1)]
        for d in ds:
            rows = a if d == -3 else jnp.where(odd == 1, b, a) if d < 0 else b if d < 2 else jnp.where(odd == 1, c, b) if d < 4 else c
            value = jnp.where(place16 == d % 4, rows, 0.0)
            value = value + swapped(value, 1)
            value = value + swapped(value, 2)
            pe2[g, d + 3, pl.ds(0, MSG, stride=2), :] = value
            pe2[g, d + 3, pl.ds(1, MSG, stride=2), :] = value

    even24 = (lanes(24) & 1) == 0

    def packed(a, b):
        return jnp.where(even24, a, b)

    def unpacked(value):
        return jnp.where(even24, value, turn(value, 1, 1)), jnp.where(even24, turn(value, -1, 1), value)

    def put_pe1(q, value):
        pe1[q + 4, pl.ds(8, 24, stride=2), :] = value
        pe1[q + 4, pl.ds(9, 24, stride=2), :] = value
        pe1[q + 4, 7:8, :] = value[23:24]
        pe1[q + 4, 56:57, :] = value[0:1]

    def correct_level1(g, reach):
        u = {q: pe2[g, q // 2 + 3, 0:24, :] for q in range(-reach - 1, 5 + reach)}
        return {
            q: KEEP * u[q] + (SIDE[1] * inside(q, 4)) * total([u[q - 1], u[q + 1], in_plane(u[q], 2)])
            for q in range(-reach, 4 + reach)
        }

    def base_level1(planes):
        answer = {}
        for q in planes:
            here = PULL[1] * f1[q + 3]
            sides = total([PULL[1] * f1[q + 2], PULL[1] * f1[q + 4], in_plane(here, 2)])
            answer[q] = (KEEP + 1.0) * here + (SIDE[1] * inside(q, 4)) * sides
        return answer

    def smooth(at, planes, plane, source):
        flag = inside(plane, 8)
        near = [at(p)[0] for p in (plane - 1, plane + 1) if p in planes]
        terms = []
        if plane in planes:
            here, before, after = at(plane)
            near += [before, after, turn(here, 1, 1) + turn(here, -1, 1)]
            terms.append(KEEP * here)
        if plane in source:
            terms.append((PULL[0] * flag) * f[plane + 3, 8:56, :])
        return total(terms + [(SIDE[0] * flag) * total(near)])

    def rows_at(ref, slot):
        return ref[slot, 8:56, :], ref[slot, 7:55, :], ref[slot, 9:57, :]

    def at_v2(p):
        return rows_at(v2, p + 4)

    def at_v(p):
        return rows_at(v, p + 6)

    def at_v1(p):
        return rows_at(v1, p + 6)

    def at_coarse(p):
        return rows_at(pe1, p // 2 + 4)

    def residual_mean(q, planes, source):
        pair = [fine_rows(v1, p + 6) for p in (2 * q, 2 * q + 1) if p in planes]
        beyond = [fine_rows(v1, p + 6) for p in (2 * q - 1, 2 * q + 2) if p in planes]
        rows = [fine_rows(f, p + 3)[:2] for p in (2 * q, 2 * q + 1) if p in source]
        return restricted(pair, beyond, rows, -CENTRE[0], STEP[0], 1)

    slab = range(8)
    for q in range(-1, 5):
        pair = [fine_rows(f, p + 3) for p in (2 * q, 2 * q + 1) if p in slab]
        beyond = [fine_rows(f, p + 3) for p in (2 * q - 1, 2 * q + 2) if p in slab]
        put_src1(q + 4, restricted(pair, beyond, [], KEEP, SIDE[0] * inside(q, 4), 1))
    send_first(level2_parts(range(-1, 5), range(-1, 3)))
    parts = {q: src1[q + 4, 8:32, :] for q in range(-1, 5)}
    for i in range(3):
        f1_out[i] = packed(parts[2 * i - 1], parts[2 * i])
    @pl.when(leads)
    def _():
        for copy in to_before:
            copy.start()

    @pl.when((core == 0) & (o != 0))
    def _():
        orb_n[...] = orb_x[...]
        occ_n[...] = occ_x[...]

    @pl.when(start)
    def _():
        orb_n[...] = orb_y[...]
        occ_n[...] = occ_y[...]

    below2, above2 = lax.rem(s + n_slab - 2, n_slab), lax.rem(s + 2, n_slab)
    send(f1_out.at[pl.ds(0, 2)], f1_in.at[pl.ds(2, 2)], f1_send.at[0], f1_recv.at[0], at_slab(below))
    send(f1_out.at[pl.ds(1, 2)], f1_in.at[pl.ds(0, 2)], f1_send.at[1], f1_recv.at[1], at_slab(above))

    send(f.at[pl.ds(3, 3), pl.ds(8, NY)], f.at[pl.ds(11, 3), pl.ds(8, NY)], f_send.at[0], f_recv.at[0], at_slab(below))
    send(f.at[pl.ds(8, 3), pl.ds(8, NY)], f.at[pl.ds(0, 3), pl.ds(8, NY)], f_send.at[1], f_recv.at[1], at_slab(above))
    faces = pending[2:4]
    pulled = {q: PULL[1] * parts[q] for q in parts}
    for q in range(-2, 6):
        near = [pulled.get(q - 1), pulled.get(q + 1)]
        terms = []
        if q in parts:
            near.append(in_plane(pulled[q], 2))
            terms = [(KEEP + 1.0) * pulled[q]]
        put_pe1(q, total(terms + [(SIDE[1] * inside(q, 4)) * total(near)]))
    for p in range(-4, 12):
        put(v2, p + 4, PULL[0] * f[p + 3, 8:56, :] + at_coarse(p)[0] if p in slab else at_coarse(p)[0])
    for p in range(-5, 13):
        put(v, p + 6, smooth(at_v2, range(-4, 12), p, slab))
    for p in range(-6, 14):
        put(v1, p + 6, smooth(at_v, range(-5, 13), p, slab))
    for q in range(-4, 8):
        put_src1(q + 4, inside(q, 4) * residual_mean(q, range(-6, 14), slab))
    shares = {q: src1[q + 4, 8:32, :] for q in (-4, -3, -2, -1, 2, 3, 0, 1, 4, 5, 6, 7)}
    for i, q in enumerate((-4, 0, 2, 6)):
        f2_out[i] = packed(shares[q], shares[q + 1])
    for i, device in enumerate((below2, below, above, above2)):
        send(f2_out.at[i], f2_in.at[i], f1_send.at[2 + i], f1_recv.at[2 + i], at_slab(device))
    send_second(level2_parts(range(-4, 8), range(-3, 5)))

    pending[0].wait_recv()
    pending[1].wait_recv()
    under = [low * plane for i in range(2) for plane in unpacked(f1_in[i])]
    over = [high * plane for i in range(2, 4) for plane in unpacked(f1_in[i])]
    mixed = {q: [part] for q, part in parts.items()}
    for first_plane, planes in ((-3, under), (3, over)):
        for i, plane in enumerate(planes):
            mixed.setdefault(first_plane + i, []).append(plane)
    for q in range(-3, 7):
        f1[q + 3] = total(mixed[q])
    base = base_level1(range(-2, 6))
    for q in base:
        e1[q + 2] = base[q]

    gathered(0).wait_recv()
    first = solve_level2(first_source())
    for y in range(12):
        e2[24 * y + 8 : 24 * y + 16, :] = first[y]
    answer = response(first)
    spread_level2(0, range(-3, 5))
    answer1 = correct_level1(0, 4)
    for q in range(-2, 6):
        put_pe1(q, answer1[q] + e1[q + 2])
    for face in faces:
        face.wait_recv()
    for p in range(-3, 11):
        put(v2, p + 4, (PULL[0] * inside(p, 8)) * f[p + 3, 8:56, :] + at_coarse(p)[0])
    for p in range(-2, 10):
        put(v, p + 6, smooth(at_v2, range(-3, 11), p, range(-3, 11)))
    for p in range(-1, 9):
        put(v1, p + 6, smooth(at_v, range(-2, 10), p, range(-3, 11)))
    weight_x = -occ_x[0:1, :]
    to_x = []
    for h in range(4):
        for p in range(2 * h, 2 * h + 2):
            last[p] = smooth(at_v1, range(-1, 9), p, slab)
            both_x[0, p] = (last[p] * weight_x) * orb_x[p]
        planes = pl.ds(2 * h, 2)
        to_x.append(remote(both_x.at[0, planes], both_x.at[1, planes], prev_send.at[h], prev_recv.at[h], before))

        @pl.when(leads)
        def _():
            to_x[h].start()

    @pl.when(start)
    def _():
        weight_y = -occ_y[0:1, :]
        for p in range(8):
            both_x[1, p] = (last[p] * weight_y) * orb_y[p]

    for q in range(4):
        f1[q + 3] = residual_mean(q, range(-1, 9), slab)

    for copy in pending[4:8]:
        copy.wait_recv()
    gathered(1).wait_recv()
    second = solve_level2([a + b for a, b in zip(answer, second_source())])
    for y in range(12):
        e2b[24 * y + 8 : 24 * y + 16, :] = second[y]
    for q in answer1:
        put_pe1(q, answer1[q])
    for lowest in (-6, 6):
        for p in range(lowest, lowest + 8):
            put(v, p + 6, smooth(at_coarse, range(-8, 16), p, ()))
        for p in range(lowest + 1, lowest + 7):
            put(v1, p + 6, smooth(at_v, range(lowest, lowest + 8), p, ()))
    own_part = {q: inside(q, 4) * residual_mean(q, range(-6, 14), ()) for q in (-2, -1, 4, 5)}
    for q, near, far, near_flag, far_flag in ((-2, 2, 3, low, low2), (4, 1, 0, high, high2)):
        for i, (a, b) in enumerate(zip(unpacked(f2_in[near]), unpacked(f2_in[far]))):
            f1[q + i + 3] = total([shares[q + i], own_part[q + i], near_flag * a, far_flag * b])
    spread_level2(1, range(-1, 3))
    answer1 = correct_level1(1, 1)
    base = base_level1(range(-1, 5))
    fixes = {q: answer1[q] + base[q] for q in answer1}
    for i in range(3):
        fix_out[i] = packed(fixes[2 * i - 1], fixes[2 * i])
    fix_copy = remote(fix_out, fix_in, before_send.at[2], before_recv.at[2], before)

    @pl.when(leads)
    def _():
        fix_copy.start()

    @pl.when(core == 0)
    def _():
        fix_in[...] = fix_out[...]

    for q in fixes:
        put_pe1(q, fixes[q])

    weight_y = -occ_y[0:1, :]
    to_y = []
    for h in range(4):
        for p in range(2 * h, 2 * h + 2):
            potential = last[p] + smooth(at_coarse, range(-2, 10), p, ())
            out_y[p] = (potential * weight_y) * orb_y[p]

            @pl.when(home)
            def _():
                in_y[p] = (potential * weight_x) * orb_x[p]

        planes = pl.ds(2 * h, 2)
        to_y.append(remote(out_y.at[planes], in_y.at[planes], ret_send.at[h], ret_recv.at[h], partner))

        @pl.when(jnp.logical_not(start))
        def _():
            to_y[h].start()

    @pl.when(core == 1)
    def _():
        for copy in to_before + to_x:
            copy.wait_recv()
        fix_copy.wait_recv()

    for i in range(3):
        for q, plane in zip((2 * i - 1, 2 * i), unpacked(fix_in[i])):
            put_pe1(q, plane)
    weight_n = -occ_n[0:1, :]
    kept = jnp.where(start, 1, core)
    for p in range(8):
        both_x[kept, p] = both_x[kept, p] + (smooth(at_coarse, range(-2, 10), p, ()) * weight_n) * orb_n[p]
    for h in range(4):

        @pl.when(jnp.logical_not(home))
        def _():
            to_y[h].wait_recv()

        for p in range(2 * h, 2 * h + 2):
            out_ref[0, p] = in_y[p] + both_x[kept, p]

    for copy in pending:
        copy.wait_send()

    @pl.when(jnp.logical_not(home))
    def _():
        for copy in to_partner:
            copy.wait_send()

    @pl.when(jnp.logical_not(start))
    def _():
        for copy in to_y:
            copy.wait_send()

    for g in range(2):
        gathered(g).wait_send()

    @pl.when(core == 1)
    def _():
        for copy in to_next:
            copy.wait_send()

    @pl.when(leads)
    def _():
        for copy in to_x + to_before + [fix_copy]:
            copy.wait_send()


def on_device(n_orb, n_slab, orbitals, occupations):
    vmem, dma = pltpu.VMEM, pltpu.SemaphoreType.DMA
    f32 = jnp.float32

    def fine(planes):
        return vmem((planes, NY, NX), f32)

    def tall(planes):
        return vmem((planes, FINE, NX), f32)

    return pl.pallas_call(
        functools.partial(kernel, n_orb, n_slab),
        out_shape=jax.ShapeDtypeStruct(orbitals.shape, f32),
        in_specs=[pl.BlockSpec(memory_space=pltpu.SMEM), pl.BlockSpec(memory_space=pltpu.HBM)],
        out_specs=pl.BlockSpec(memory_space=pltpu.VMEM),
        scratch_shapes=[
            fine(8), fine(8), fine(8), vmem((8, 128), f32), vmem((8, 128), f32), vmem((8, 128), f32),
            tall(14), tall(16), tall(20), tall(20), tall(12),
            vmem((10, 24, 128), f32), vmem((12, ROWS1, 128), f32), vmem((2, 8, 32, 128), f32), vmem((8, 24, 128), f32),
            vmem((3, 24, 128), f32), vmem((4, 24, 128), f32), vmem((4, 24, 128), f32), vmem((4, 24, 128), f32), vmem((MSG2, 128), f32),
            vmem((18 * MSG, 128), f32), vmem((20 * MSG2, 128), f32), vmem((24 * 16, 128), f32), vmem((24 * 16, 128), f32),
            fine(8), fine(8), vmem((2, 8, NY, NX), f32),
            fine(8), vmem((8, 128), f32), fine(8), vmem((3, 24, 128), f32), vmem((3, 24, 128), f32),
            pltpu.SemaphoreType.REGULAR, dma, dma((2,)), dma((2,)), dma((2,)), dma((2,)), dma((2,)), dma((2,)), dma((6,)), dma((6,)), dma((2,)), dma((2,)),
            dma((4,)), dma((4,)), dma((4,)), dma((4,)), dma((3,)), dma((3,)),
        ],
        compiler_params=pltpu.CompilerParams(collective_id=0, has_side_effects=True, vmem_limit_bytes=32 * 2**20),
    )(occupations, pltpu.with_memory_space_constraint(orbitals, pltpu.HBM))


def solution(mesh):
    return jax.shard_map(
        functools.partial(on_device, mesh.shape["orb"], mesh.shape["slab"]),
        mesh=mesh,
        in_specs=(P("orb", "slab", None, None), P("orb")),
        out_specs=P("orb", "slab", None, None),
        check_vma=False,
    )
```

profile of v0, /device:TPU:97, one launch (start us, length us, event | category | flops | bytes accessed | tf_op | source)
XLA Modules:
  0.0 23.9 jit_solution(4660068143240420758)
XLA Ops:
  0.7 22.6 %shard_map.28 = f32[1,8,48,128]{3,2,1,0:T(8,128)S(1)} custom-call(f32[1]{0:T(128)S(6)} %copy.4.occ_ref, f32[1,8,48,128]{3,2,1,0:T(8,128)} %orb_ref.1), custom_call_target="tpu_custom_call" | custom-call | tf_op jit(solution)/shard_map/pallas_call | solution.py:679
  23.2 0.7 %copy.5 = f32[1,8,48,128]{3,2,1,0:T(8,128)} copy(f32[1,8,48,128]{3,2,1,0:T(8,128)S(1)} %shard_map.28) | data formatting | bytes 393216
where the time goes:
time: 24 us; the launch traced here: 23.9 us
  Pallas kernels  22.6 us (94%)
  local copies, waits for them, and re-layouts  0.68 us (3%)
  between operations  0.66 us (3%)
    pallas_call x1, Pallas kernels, on_device(): pl.pallas_call(functools.partial(kernel, n_orb, n_slab), out_shape=jax.Sh...  22.6 us
    unnamed x1, local copies, waits for them, and re-layouts  0.68 us

commit v1 on v0

--- a/solution.py
+++ b/solution.py
@@ -449,6 +449,12 @@
 
     def at_coarse(p):
         return rows_at(pe1, p // 2 + 4)
+
+    def smooth_coarse(q):
+        here, before, after = at_coarse(2 * q)
+        side = SIDE[0] * inside(q, 4)
+        inner = KEEP * here + side * total([here, before, after, turn(here, 1, 1), turn(here, -1, 1)])
+        return inner + side * at_coarse(2 * q - 2)[0], inner + side * at_coarse(2 * q + 2)[0]
 
     def residual_mean(q, planes, source):
         pair = [fine_rows(v1, p + 6) for p in (2 * q, 2 * q + 1) if p in planes]
@@ -572,8 +578,9 @@
     for q in answer1:
         put_pe1(q, answer1[q])
     for lowest in (-6, 6):
-        for p in range(lowest, lowest + 8):
-            put(v, p + 6, smooth(at_coarse, range(-8, 16), p, ()))
+        for q in range(lowest // 2, lowest // 2 + 4):
+            for p, plane in zip((2 * q, 2 * q + 1), smooth_coarse(q)):
+                put(v, p + 6, plane)
         for p in range(lowest + 1, lowest + 7):
             put(v1, p + 6, smooth(at_v, range(lowest, lowest + 8), p, ()))
     own_part = {q: inside(q, 4) * residual_mean(q, range(-6, 14), ()) for q in (-2, -1, 4, 5)}
@@ -602,8 +609,8 @@
     weight_y = -occ_y[0:1, :]
     to_y = []
     for h in range(4):
-        for p in range(2 * h, 2 * h + 2):
-            potential = last[p] + smooth(at_coarse, range(-2, 10), p, ())
+        for p, fix in zip((2 * h, 2 * h + 1), smooth_coarse(h)):
+            potential = last[p] + fix
             out_y[p] = (potential * weight_y) * orb_y[p]
 
             @pl.when(home)
@@ -628,8 +635,9 @@
             put_pe1(q, plane)
     weight_n = -occ_n[0:1, :]
     kept = jnp.where(start, 1, core)
-    for p in range(8):
-        both_x[kept, p] = both_x[kept, p] + (smooth(at_coarse, range(-2, 10), p, ()) * weight_n) * orb_n[p]
+    for h in range(4):
+        for p, fix in zip((2 * h, 2 * h + 1), smooth_coarse(h)):
+            both_x[kept, p] = both_x[kept, p] + (fix * weight_n) * orb_n[p]
     for h in range(4):
 
         @pl.when(jnp.logical_not(home))
@@ -684,9 +692,9 @@
         scratch_shapes=[
             fine(8), fine(8), fine(8), vmem((8, 128), f32), vmem((8, 128), f32), vmem((8, 128), f32),
             tall(14), tall(16), tall(20), tall(20), tall(12),
-            vmem((10, 24, 128), f32), vmem((12, ROWS1, 128), f32), vmem((2, 8, 32, 128), f32), vmem((8, 24, 128), f32),
+            vmem((10, 24, 128), f32), vmem((12, ROWS1, 128), f32), vmem((2, 8, 40, 128), f32), vmem((8, 24, 128), f32),
             vmem((3, 24, 128), f32), vmem((4, 24, 128), f32), vmem((4, 24, 128), f32), vmem((4, 24, 128), f32), vmem((MSG2, 128), f32),
-            vmem((18 * MSG, 128), f32), vmem((20 * MSG2, 128), f32), vmem((24 * 16, 128), f32), vmem((24 * 16, 128), f32),
+            vmem((20 * MSG, 128), f32), vmem((22 * MSG2, 128), f32), vmem((24 * 17, 128), f32), vmem((24 * 17, 128), f32),
             fine(8), fine(8), vmem((2, 8, NY, NX), f32),
             fine(8), vmem((8, 128), f32), fine(8), vmem((3, 24, 128), f32), vmem((3, 24, 128), f32),
             pltpu.SemaphoreType.REGULAR, dma, dma((2,)), dma((2,)), dma((2,)), dma((2,)), dma((2,)), dma((2,)), dma((6,)), dma((6,)), dma((2,)), dma((2,)),

time: 24 us -> 24 us (level)
  no operation moved by 1% of the time
where the time goes in v1:
time: 24 us; the launch traced here: 23.9 us
  Pallas kernels  22.5 us (94%)
  local copies, waits for them, and re-layouts  0.68 us (3%)
  between operations  0.66 us (3%)
    pallas_call x1, Pallas kernels, on_device(): pl.pallas_call(functools.partial(kernel, n_orb, n_slab), out_shape=jax.Sh...  22.5 us
    unnamed x1, local copies, waits for them, and re-layouts  0.68 us

profile of v1, /device:TPU:97, one launch (start us, length us, event | category | flops | bytes accessed | tf_op | source)
XLA Modules:
  0.0 23.9 jit_solution(8915147667122431277)
XLA Ops:
  0.7 22.5 %shard_map.28 = f32[1,8,48,128]{3,2,1,0:T(8,128)S(1)} custom-call(f32[1]{0:T(128)S(6)} %copy.4.occ_ref, f32[1,8,48,128]{3,2,1,0:T(8,128)} %orb_ref.1), custom_call_target="tpu_custom_call" | custom-call | tf_op jit(solution)/shard_map/pallas_call | solution.py:687
  23.2 0.7 %copy.5 = f32[1,8,48,128]{3,2,1,0:T(8,128)} copy(f32[1,8,48,128]{3,2,1,0:T(8,128)S(1)} %shard_map.28) | data formatting | bytes 393216

commit v2 on v0

--- a/solution.py
+++ b/solution.py
@@ -684,9 +684,9 @@
         scratch_shapes=[
             fine(8), fine(8), fine(8), vmem((8, 128), f32), vmem((8, 128), f32), vmem((8, 128), f32),
             tall(14), tall(16), tall(20), tall(20), tall(12),
-            vmem((10, 24, 128), f32), vmem((12, ROWS1, 128), f32), vmem((2, 8, 32, 128), f32), vmem((8, 24, 128), f32),
+            vmem((10, 24, 128), f32), vmem((12, ROWS1, 128), f32), vmem((2, 8, 40, 128), f32), vmem((8, 24, 128), f32),
             vmem((3, 24, 128), f32), vmem((4, 24, 128), f32), vmem((4, 24, 128), f32), vmem((4, 24, 128), f32), vmem((MSG2, 128), f32),
-            vmem((18 * MSG, 128), f32), vmem((20 * MSG2, 128), f32), vmem((24 * 16, 128), f32), vmem((24 * 16, 128), f32),
+            vmem((20 * MSG, 128), f32), vmem((22 * MSG2, 128), f32), vmem((24 * 17, 128), f32), vmem((24 * 17, 128), f32),
             fine(8), fine(8), vmem((2, 8, NY, NX), f32),
             fine(8), vmem((8, 128), f32), fine(8), vmem((3, 24, 128), f32), vmem((3, 24, 128), f32),
             pltpu.SemaphoreType.REGULAR, dma, dma((2,)), dma((2,)), dma((2,)), dma((2,)), dma((2,)), dma((2,)), dma((6,)), dma((6,)), dma((2,)), dma((2,)),

time: 24 us -> 24 us (level)
  no operation moved by 1% of the time
where the time goes in v2:
time: 24 us; the launch traced here: 23.9 us
  Pallas kernels  22.6 us (94%)
  local copies, waits for them, and re-layouts  0.68 us (3%)
  between operations  0.66 us (3%)
    pallas_call x1, Pallas kernels, on_device(): pl.pallas_call(functools.partial(kernel, n_orb, n_slab), out_shape=jax.Sh...  22.6 us
    unnamed x1, local copies, waits for them, and re-layouts  0.68 us

profile of v2, /device:TPU:97, one launch (start us, length us, event | category | flops | bytes accessed | tf_op | source)
XLA Modules:
  0.0 23.9 jit_solution(7320603321535368138)
XLA Ops:
  0.7 22.6 %shard_map.28 = f32[1,8,48,128]{3,2,1,0:T(8,128)S(1)} custom-call(f32[1]{0:T(128)S(6)} %copy.4.occ_ref, f32[1,8,48,128]{3,2,1,0:T(8,128)} %orb_ref.1), custom_call_target="tpu_custom_call" | custom-call | tf_op jit(solution)/shard_map/pallas_call | solution.py:679
  23.2 0.7 %copy.5 = f32[1,8,48,128]{3,2,1,0:T(8,128)} copy(f32[1,8,48,128]{3,2,1,0:T(8,128)S(1)} %shard_map.28) | data formatting | bytes 393216
